TPU v7x, 256 devices: a whole 4x4x8 slice. The times are simulated.
256 devices in a mesh: stretch: 32 (over z, x_hi, core), head: 8 (over x_lo, y).
Axes of the slice: x: 4 (x_hi: 2, x_lo: 2; x = x_hi * 2 + x_lo), y: 4, z: 8, core: 2. Of those that a mesh axis runs over, the one named last changes fastest.
Arguments:
- queries: bfloat16 [32768, 3072], P(('stretch', 'head')), as said below
- keys: bfloat16 [32768, 3072], P(('stretch', 'head')), as said below
- values: bfloat16 [32768, 3072], P(('stretch', 'head')), may hold values from -6 to 6
- visible: int32 [32], replicated, may hold values from 0 to 4, as said below
- lengths: int32 [32], replicated, may hold values from 512 to 1024, as said below
Outputs:
- attended: bfloat16 [32768, 3072], P(('stretch', 'head'))
Inputs may be any that keep to these rules, and one draw needn't show every extreme that they name: `queries`: every entry lies in -5 to 5. `keys`: every entry lies in -5 to 5. Some stretch at index 4 or later has visible = 4. `lengths`: some stretch is full.
All inputs are finite; a program needn't handle non-finite values.
Results may differ from a plain program's by a relative error of at most 0.0047.
Values may be sent and summed in bfloat16 or wider, within the bound.
No kernel may reach another device: no remote copies, remote signals or barrier semaphores. Data moves between devices by JAX's collectives and lax.ppermute only.
A program may use at most 128 MiB of HBM per device.

v0:
```python
import jax
import jax.numpy as jnp
from jax import lax
from jax.sharding import PartitionSpec as P

HEAD_DIM = 128
SPAN = 4


def from_behind(block, axis, distance):
    devices = range(lax.axis_size(axis))
    route = [(i - distance, i) for i in devices if i - distance in devices]
    return lax.ppermute(block, axis, route)


def reach_back(pair):
    earlier = [from_behind((pair[0], pair[1]), "stretch", back) for back in range(1, SPAN + 1)]
    return earlier


def on_device(queries, keys, values, visible, lengths):
    stretch_id = lax.axis_index("stretch")
    query_heads, key_heads, value_heads = (
        lax.all_to_all(queries, "head", split_axis=1, concat_axis=0, tiled=True),
        lax.all_to_all(keys, "head", split_axis=1, concat_axis=0, tiled=True),
        lax.all_to_all(values, "head", split_axis=1, concat_axis=0, tiled=True),
    )
    earlier = reach_back((key_heads, value_heads))
    stretch_rows = query_heads.shape[0]
    local_width = query_heads.shape[1]
    head_count = local_width // HEAD_DIM
    places = jnp.arange(stretch_rows, dtype=jnp.int32)
    usable_parts = [places < lengths[stretch_id]]
    for back in range(1, SPAN + 1):
        source = jnp.maximum(stretch_id - back, 0)
        seen = back <= jnp.minimum(visible[stretch_id], stretch_id)
        usable_parts.append(jnp.logical_and(seen, places < lengths[source]))
    usable = jnp.concatenate(usable_parts, 0)
    key_all = jnp.concatenate([key_heads] + [item[0] for item in earlier], 0).reshape(
        -1, head_count, HEAD_DIM
    )
    value_all = jnp.concatenate([value_heads] + [item[1] for item in earlier], 0).reshape(
        -1, head_count, HEAD_DIM
    )
    block_rows = min(512, stretch_rows)
    query_blocks = query_heads.reshape(stretch_rows // block_rows, block_rows, head_count, HEAD_DIM)

    def attend(query_block):
        scores = jnp.einsum(
            "qhd,khd->hqk", query_block, key_all, preferred_element_type=jnp.float32
        ) * HEAD_DIM ** (-0.5)
        scores = jnp.where(usable[None, None, :], scores, -jnp.inf)
        largest = jnp.max(scores, axis=2, keepdims=True)
        weights = jnp.exp(scores - largest)
        total = jnp.sum(weights, axis=2)
        rounded = weights.astype(jnp.bfloat16)
        mixed = jnp.einsum("hqk,khd->qhd", rounded, value_all, preferred_element_type=jnp.float32)
        return mixed / jnp.transpose(total)[:, :, None]

    mixed = lax.map(attend, query_blocks).reshape(stretch_rows, head_count, HEAD_DIM)
    mixed = jnp.where((places < lengths[stretch_id])[:, None, None], mixed, 0.0)
    outgoing = mixed.reshape(stretch_rows, local_width).astype(jnp.bfloat16)
    return lax.all_to_all(outgoing, "head", split_axis=0, concat_axis=1, tiled=True)


def solution(mesh):
    placed = (
        P(("stretch", "head"), None),
        P(("stretch", "head"), None),
        P(("stretch", "head"), None),
        P(),
        P(),
    )
    return jax.shard_map(
        on_device,
        mesh=mesh,
        in_specs=placed,
        out_specs=P(("stretch", "head"), None),
        check_vma=False,
    )
```

profile of v0, /device:TPU:69, one launch (start us, length us, event | category | flops | bytes accessed | tf_op | source)
XLA Modules:
  0.0 294.5 jit_solution(17527347797137571073)
XLA Ops:
  0.0 2.4 copy.51
  2.4 4.8 %all-to-all-start.2 = ((bf16[128,8,384]{0,2,1:T(8,128)(2,1)}), bf16[128,8,384]{0,2,1:T(8,128)(2,1)S(1)}, u32[]{:S(2)}, u32[]{:S(2)}) async-start(bf16[128,8,384]{0,2,1:T(8,128)(2,1)} %bitcast.19), calls=%async_computation.2 | async-start | bytes 1572864 | tf_op jit(solution)/shard_map/all_to_all | solution.py:26
  7.2 2.3 copy.44
  9.5 9.1 %all-to-all-done.2 = bf16[128,8,384]{0,2,1:T(8,128)(2,1)S(1)} async-done(((bf16[128,8,384]{0,2,1:T(8,128)(2,1)}), bf16[128,8,384]{0,2,1:T(8,128)(2,1)S(1)}, u32[]{:S(2)}, u32[]{:S(2)}) %all-to-all-start.2) | async-done | bytes 786464 | tf_op jit(solution)/shard_map/all_to_all | solution.py:26
  18.6 4.4 %all-to-all-start.1 = ((bf16[128,8,384]{0,2,1:T(8,128)(2,1)}), bf16[128,8,384]{0,2,1:T(8,128)(2,1)S(1)}, u32[]{:S(2)}, u32[]{:S(2)}) async-start(bf16[128,8,384]{0,2,1:T(8,128)(2,1)} %bitcast.12), calls=%async_computation.1 | async-start | bytes 1572864 | tf_op jit(solution)/shard_map/all_to_all | solution.py:25
  24.2 4.4 %collective-permute-start.4 = (bf16[1024,384]{1,0:T(8,128)(2,1)}, bf16[1024,384]{1,0:T(8,128)(2,1)}, u32[]{:S(2)}, u32[]{:S(2)}) collective-permute-start(bf16[1024,384]{1,0:T(8,128)(2,1)} %bitcast.21), channel_id=1, source_target_pairs={{0,8},{8,16},{16,24},{24,32},{32,40},{40,48},{48,56},{56,64},{64,7... | collective-permute-start | bytes 2359304 | tf_op jit(solution)/shard_map/ppermute | solution.py:13
  28.6 4.4 %collective-permute-start.5 = (bf16[1024,384]{1,0:T(8,128)(2,1)}, bf16[1024,384]{1,0:T(8,128)(2,1)}, u32[]{:S(2)}, u32[]{:S(2)}) collective-permute-start(bf16[1024,384]{1,0:T(8,128)(2,1)} %bitcast.21), channel_id=1, source_target_pairs={{0,16},{8,24},{16,32},{24,40},{32,48},{40,56},{48,64},{56,72},{64,... | collective-permute-start | bytes 2359304 | tf_op jit(solution)/shard_map/ppermute | solution.py:13
  34.2 24.3 %all-to-all-done.1 = bf16[128,8,384]{0,2,1:T(8,128)(2,1)S(1)} async-done(((bf16[128,8,384]{0,2,1:T(8,128)(2,1)}), bf16[128,8,384]{0,2,1:T(8,128)(2,1)S(1)}, u32[]{:S(2)}, u32[]{:S(2)}) %all-to-all-start.1) | async-done | bytes 786464 | tf_op jit(solution)/shard_map/all_to_all | solution.py:25
  58.4 4.0 %all-to-all-start = ((bf16[128,8,384]{0,2,1:T(8,128)(2,1)}), bf16[128,8,384]{0,2,1:T(8,128)(2,1)S(1)}, u32[]{:S(2)}, u32[]{:S(2)}) async-start(bf16[128,8,384]{0,2,1:T(8,128)(2,1)} %bitcast.10), calls=%async_computation | async-start | bytes 1572864 | tf_op jit(solution)/shard_map/all_to_all | solution.py:24
  64.9 5.7 %collective-permute-start.6 = (bf16[1024,384]{1,0:T(8,128)(2,1)}, bf16[1024,384]{1,0:T(8,128)(2,1)}, u32[]{:S(2)}, u32[]{:S(2)}) collective-permute-start(bf16[1024,384]{1,0:T(8,128)(2,1)} %bitcast.21), channel_id=1, source_target_pairs={{0,24},{8,32},{16,40},{24,48},{32,56},{40,64},{48,72},{56,80},{64,... | collective-permute-start | bytes 2359304 | tf_op jit(solution)/shard_map/ppermute | solution.py:13
  70.7 4.8 %collective-permute-start.7 = (bf16[1024,384]{1,0:T(8,128)(2,1)}, bf16[1024,384]{1,0:T(8,128)(2,1)}, u32[]{:S(2)}, u32[]{:S(2)}) collective-permute-start(bf16[1024,384]{1,0:T(8,128)(2,1)} %bitcast.21), channel_id=1, source_target_pairs={{0,32},{8,40},{16,48},{24,56},{32,64},{40,72},{48,80},{56,88},{64,... | collective-permute-start | bytes 2359304 | tf_op jit(solution)/shard_map/ppermute | solution.py:13
  81.8 2.9 collective-permute-start
  86.6 3.9 %collective-permute-start.1 = (bf16[1024,384]{1,0:T(8,128)(2,1)}, bf16[1024,384]{1,0:T(8,128)(2,1)}, u32[]{:S(2)}, u32[]{:S(2)}) collective-permute-start(bf16[1024,384]{1,0:T(8,128)(2,1)} %bitcast.76), channel_id=1, source_target_pairs={{0,16},{8,24},{16,32},{24,40},{32,48},{40,56},{48,64},{56,72},{64,... | collective-permute-start | bytes 2359304 | tf_op jit(solution)/shard_map/ppermute | solution.py:13
  90.6 1.9 collective-permute-start.2
  97.3 2.8 collective-permute-start.3
  101.5 6.3 %collective-permute-done.7 = bf16[1024,384]{1,0:T(8,128)(2,1)} collective-permute-done((bf16[1024,384]{1,0:T(8,128)(2,1)}, bf16[1024,384]{1,0:T(8,128)(2,1)}, u32[]{:S(2)}, u32[]{:S(2)}) %collective-permute-start.7) | collective-permute-done | bytes 786464 | tf_op jit(solution)/shard_map/ppermute | solution.py:13
  107.8 2.3 copy.57
  114.1 6.2 %copy.60 = bf16[5120,3,128]{2,0,1:T(8,128)(2,1)} copy(bf16[5120,3,128]{0,2,1:T(8,128)(2,1)} %constant_dynamic-update-slice_fusion.6) | data formatting | bytes 7864320 | tf_op jit(solution)/shard_map/while | solution.py:60
  123.5 15.4 %collective-permute-done.1 = bf16[1024,384]{1,0:T(8,128)(2,1)} collective-permute-done((bf16[1024,384]{1,0:T(8,128)(2,1)}, bf16[1024,384]{1,0:T(8,128)(2,1)}, u32[]{:S(2)}, u32[]{:S(2)}) %collective-permute-start.1) | collective-permute-done | bytes 786464 | tf_op jit(solution)/shard_map/ppermute | solution.py:13
  140.3 14.1 %collective-permute-done.2 = bf16[1024,384]{1,0:T(8,128)(2,1)} collective-permute-done((bf16[1024,384]{1,0:T(8,128)(2,1)}, bf16[1024,384]{1,0:T(8,128)(2,1)}, u32[]{:S(2)}, u32[]{:S(2)}) %collective-permute-start.2) | collective-permute-done | bytes 786464 | tf_op jit(solution)/shard_map/ppermute | solution.py:13
  158.8 10.2 %collective-permute-done.3 = bf16[1024,384]{1,0:T(8,128)(2,1)} collective-permute-done((bf16[1024,384]{1,0:T(8,128)(2,1)}, bf16[1024,384]{1,0:T(8,128)(2,1)}, u32[]{:S(2)}, u32[]{:S(2)}) %collective-permute-start.3) | collective-permute-done | bytes 786464 | tf_op jit(solution)/shard_map/ppermute | solution.py:13
  171.5 6.3 %copy.59 = bf16[5120,3,128]{2,0,1:T(8,128)(2,1)} copy(bf16[5120,3,128]{0,2,1:T(8,128)(2,1)} %constant_dynamic-update-slice_fusion.1) | data formatting | bytes 7864320 | tf_op jit(solution)/shard_map/while | solution.py:60
  177.8 100.9 %while.10 = (s32[]{:T(128)}, bf16[2,512,3,128]{1,0,3,2:T(2,128)(2,1)S(1)}, pred[5120]{0:T(1024)(128)(4,1)S(1)}, bf16[2,512,3,128]{3,1,2,0:T(8,128)(2,1)S(1)}, bf...) while((s32[]{:T(128)}, bf16[2,512,3,128]{1,0,3,2:T(2,128)(2,1)S(1)}, ...), condition=%wide.region_3.4_spmd, body=%wide.region_0.3_spmd.sunk | while | flops 4113429504 | bytes 120370296 | solution.py:60
  177.8 14.7 %fusion.37 = (f32[3,512]{1,0:T(4,128)S(1)}, f32[3,512,5120]{2,1,0:T(8,128)}) fusion(pred[5120]{0:T(1024)(128)(4,1)S(1)} %get-tuple-element.134, bf16[5120,3,128]{2,0,1:T(8,128)(2,1)} %get-tuple-element.136, bf16[2,512,3,128]{3,1,2,0:T(8,128)(2,1)S(1)} %get-tuple-element.135, s32[]{:T(128)} %get-tuple-element.124), kind=kOutput, calls=%fused_computation.2.clone.1 | convolution fusion | flops 2036857344 | bytes 35793924 | tf_op jit(solution)/shard_map/while/body/eval_jaxpr/qhd,khd->hqk/dot_general | solution.py:49
  192.5 14.3 %fusion.38 = f32[3,512]{1,0:T(4,128)S(1)} fusion(f32[3,512,5120]{2,1,0:T(8,128)} %get-tuple-element.114, f32[3,512]{1,0:T(4,128)S(1)} %get-tuple-element.115, pred[5120]{0:T(1024)(128)(4,1)S(1)} %get-tuple-element.134), kind=kLoop, calls=%fused_computation.3.clone.1 | loop fusion | flops 31455744 | bytes 31474688 | tf_op jit(solution)/shard_map/while/body/eval_jaxpr/reduce_sum | solution.py:55
  206.8 13.8 %fusion.39 = bf16[1,512,3,128]{3,1,2,0:T(8,128)(2,1)S(1)} fusion(bf16[5120,3,128]{2,0,1:T(8,128)(2,1)S(1)} %copy-done, f32[3,512,5120]{2,1,0:T(8,128)} %get-tuple-element.114, f32[3,512]{1,0:T(4,128)S(1)} %get-tuple-element.115, pred[5120]{0:T(1024)(128)(4,1)S(1)} %get-tuple-element.134, f32[512,3]{0,1:T(4,128)S(1)} %bitcast.79), kind=kOutput, calls=%fused_computation.9.clone.1 | convolution fusion | flops 2045116416 | bytes 35800064 | tf_op jit(solution)/shard_map/while/body/eval_jaxpr/hqk,khd->qhd/dot_general | solution.py:57
  221.2 7.0 %dynamic_update_slice.5 = bf16[2,512,3,128]{1,0,3,2:T(2,128)(2,1)S(1)} dynamic-update-slice(bf16[2,512,3,128]{1,0,3,2:T(2,128)(2,1)S(1)} %get-tuple-element.125, bf16[1,512,3,128]{1,0,3,2:T(2,128)(2,1)S(1)} %copy.67, s32[]{:T(128)} %get-tuple-element.124, s32[]{:T(128)} %constant.39.clone.1..sunk, s32[]{:T(128)} %constant.39.clone.1..sunk, s32[]{:T(128)} %constant.39.clone.1..sunk) | dynamic-update-slice | bytes 786436 | tf_op jit(solution)/shard_map/while/body/jit(dynamic_update_index_in_dim)/dynamic_update_slice | solution.py:60
  228.2 14.7 %fusion.37 = (f32[3,512]{1,0:T(4,128)S(1)}, f32[3,512,5120]{2,1,0:T(8,128)}) fusion(pred[5120]{0:T(1024)(128)(4,1)S(1)} %get-tuple-element.134, bf16[5120,3,128]{2,0,1:T(8,128)(2,1)} %get-tuple-element.136, bf16[2,512,3,128]{3,1,2,0:T(8,128)(2,1)S(1)} %get-tuple-element.135, s32[]{:T(128)} %get-tuple-element.124), kind=kOutput, calls=%fused_computation.2.clone.1 | convolution fusion | flops 2036857344 | bytes 35793924 | tf_op jit(solution)/shard_map/while/body/eval_jaxpr/qhd,khd->hqk/dot_general | solution.py:49
  242.9 14.3 %fusion.38 = f32[3,512]{1,0:T(4,128)S(1)} fusion(f32[3,512,5120]{2,1,0:T(8,128)} %get-tuple-element.114, f32[3,512]{1,0:T(4,128)S(1)} %get-tuple-element.115, pred[5120]{0:T(1024)(128)(4,1)S(1)} %get-tuple-element.134), kind=kLoop, calls=%fused_computation.3.clone.1 | loop fusion | flops 31455744 | bytes 31474688 | tf_op jit(solution)/shard_map/while/body/eval_jaxpr/reduce_sum | solution.py:55
  257.2 13.8 %fusion.39 = bf16[1,512,3,128]{3,1,2,0:T(8,128)(2,1)S(1)} fusion(bf16[5120,3,128]{2,0,1:T(8,128)(2,1)S(1)} %copy-done, f32[3,512,5120]{2,1,0:T(8,128)} %get-tuple-element.114, f32[3,512]{1,0:T(4,128)S(1)} %get-tuple-element.115, pred[5120]{0:T(1024)(128)(4,1)S(1)} %get-tuple-element.134, f32[512,3]{0,1:T(4,128)S(1)} %bitcast.79), kind=kOutput, calls=%fused_computation.9.clone.1 | convolution fusion | flops 2045116416 | bytes 35800064 | tf_op jit(solution)/shard_map/while/body/eval_jaxpr/hqk,khd->qhd/dot_general | solution.py:57
  271.6 7.0 %dynamic_update_slice.5 = bf16[2,512,3,128]{1,0,3,2:T(2,128)(2,1)S(1)} dynamic-update-slice(bf16[2,512,3,128]{1,0,3,2:T(2,128)(2,1)S(1)} %get-tuple-element.125, bf16[1,512,3,128]{1,0,3,2:T(2,128)(2,1)S(1)} %copy.67, s32[]{:T(128)} %get-tuple-element.124, s32[]{:T(128)} %constant.39.clone.1..sunk, s32[]{:T(128)} %constant.39.clone.1..sunk, s32[]{:T(128)} %constant.39.clone.1..sunk) | dynamic-update-slice | bytes 786436 | tf_op jit(solution)/shard_map/while/body/jit(dynamic_update_index_in_dim)/dynamic_update_slice | solution.py:60
  279.5 13.8 %all_to_all.70 = bf16[8,128,384]{1,2,0:T(8,128)(2,1)S(1)} all-to-all(bf16[8,128,384]{1,2,0:T(8,128)(2,1)S(1)} %copy.62), channel_id=1, replica_groups=mesh['stretch'=32,'head'=8] {'head'}, dimensions={0} | all-to-all | bytes 1572864 | tf_op jit(solution)/shard_map/all_to_all | solution.py:63
  (63 shorter events, 37.2 us)
Async XLA Ops:
  0.0 33.0 %copy-start.2 = (bf16[128,3072]{1,0:T(8,128)(2,1)S(1)}, bf16[128,3072]{1,0:T(8,128)(2,1)}, u32[]{:S(2)}) copy-start(bf16[128,3072]{1,0:T(8,128)(2,1)} %param.7) | copy-start | bytes 2359300
  2.4 16.2 %all-to-all-start.2 = ((bf16[128,8,384]{0,2,1:T(8,128)(2,1)}), bf16[128,8,384]{0,2,1:T(8,128)(2,1)S(1)}, u32[]{:S(2)}, u32[]{:S(2)}) async-start(bf16[128,8,384]{0,2,1:T(8,128)(2,1)} %bitcast.19), calls=%async_computation.2 | async-start | bytes 1572864 | tf_op jit(solution)/shard_map/all_to_all | solution.py:26
  7.2 55.2 %copy-start.6 = (s32[32]{0:T(128)S(1)}, s32[32]{0:T(128)}, u32[]{:S(2)}) copy-start(s32[32]{0:T(128)} %param.10) | copy-start | bytes 388
  7.2 56.4 %copy-start.4 = (s32[32]{0:T(128)S(1)}, s32[32]{0:T(128)}, u32[]{:S(2)}) copy-start(s32[32]{0:T(128)} %param.11) | copy-start | bytes 388
  18.6 39.9 %all-to-all-start.1 = ((bf16[128,8,384]{0,2,1:T(8,128)(2,1)}), bf16[128,8,384]{0,2,1:T(8,128)(2,1)S(1)}, u32[]{:S(2)}, u32[]{:S(2)}) async-start(bf16[128,8,384]{0,2,1:T(8,128)(2,1)} %bitcast.12), calls=%async_computation.1 | async-start | bytes 1572864 | tf_op jit(solution)/shard_map/all_to_all | solution.py:25
  24.2 62.4 %collective-permute-start.4 = (bf16[1024,384]{1,0:T(8,128)(2,1)}, bf16[1024,384]{1,0:T(8,128)(2,1)}, u32[]{:S(2)}, u32[]{:S(2)}) collective-permute-start(bf16[1024,384]{1,0:T(8,128)(2,1)} %bitcast.21), channel_id=1, source_target_pairs={{0,8},{8,16},{16,24},{24,32},{32,40},{40,48},{48,56},{56,64},{64,7... | collective-permute-start | bytes 2359304 | tf_op jit(solution)/shard_map/ppermute | solution.py:13
  28.6 61.9 %collective-permute-start.5 = (bf16[1024,384]{1,0:T(8,128)(2,1)}, bf16[1024,384]{1,0:T(8,128)(2,1)}, u32[]{:S(2)}, u32[]{:S(2)}) collective-permute-start(bf16[1024,384]{1,0:T(8,128)(2,1)} %bitcast.21), channel_id=1, source_target_pairs={{0,16},{8,24},{16,32},{24,40},{32,48},{40,56},{48,64},{56,72},{64,... | collective-permute-start | bytes 2359304 | tf_op jit(solution)/shard_map/ppermute | solution.py:13
  58.4 26.6 %all-to-all-start = ((bf16[128,8,384]{0,2,1:T(8,128)(2,1)}), bf16[128,8,384]{0,2,1:T(8,128)(2,1)S(1)}, u32[]{:S(2)}, u32[]{:S(2)}) async-start(bf16[128,8,384]{0,2,1:T(8,128)(2,1)} %bitcast.10), calls=%async_computation | async-start | bytes 1572864 | tf_op jit(solution)/shard_map/all_to_all | solution.py:24
  64.9 32.4 %collective-permute-start.6 = (bf16[1024,384]{1,0:T(8,128)(2,1)}, bf16[1024,384]{1,0:T(8,128)(2,1)}, u32[]{:S(2)}, u32[]{:S(2)}) collective-permute-start(bf16[1024,384]{1,0:T(8,128)(2,1)} %bitcast.21), channel_id=1, source_target_pairs={{0,24},{8,32},{16,40},{24,48},{32,56},{40,64},{48,72},{56,80},{64,... | collective-permute-start | bytes 2359304 | tf_op jit(solution)/shard_map/ppermute | solution.py:13
  70.7 37.1 %collective-permute-start.7 = (bf16[1024,384]{1,0:T(8,128)(2,1)}, bf16[1024,384]{1,0:T(8,128)(2,1)}, u32[]{:S(2)}, u32[]{:S(2)}) collective-permute-start(bf16[1024,384]{1,0:T(8,128)(2,1)} %bitcast.21), channel_id=1, source_target_pairs={{0,32},{8,40},{16,48},{24,56},{32,64},{40,72},{48,80},{56,88},{64,... | collective-permute-start | bytes 2359304 | tf_op jit(solution)/shard_map/ppermute | solution.py:13
  81.8 40.2 %collective-permute-start = (bf16[1024,384]{1,0:T(8,128)(2,1)}, bf16[1024,384]{1,0:T(8,128)(2,1)}, u32[]{:S(2)}, u32[]{:S(2)}) collective-permute-start(bf16[1024,384]{1,0:T(8,128)(2,1)} %bitcast.75), channel_id=1, source_target_pairs={{0,8},{8,16},{16,24},{24,32},{32,40},{40,48},{48,56},{56,64},{64,7... | collective-permute-start | bytes 2359304 | tf_op jit(solution)/shard_map/ppermute | solution.py:13
  86.6 52.3 %collective-permute-start.1 = (bf16[1024,384]{1,0:T(8,128)(2,1)}, bf16[1024,384]{1,0:T(8,128)(2,1)}, u32[]{:S(2)}, u32[]{:S(2)}) collective-permute-start(bf16[1024,384]{1,0:T(8,128)(2,1)} %bitcast.76), channel_id=1, source_target_pairs={{0,16},{8,24},{16,32},{24,40},{32,48},{40,56},{48,64},{56,72},{64,... | collective-permute-start | bytes 2359304 | tf_op jit(solution)/shard_map/ppermute | solution.py:13
  90.6 63.9 %collective-permute-start.2 = (bf16[1024,384]{1,0:T(8,128)(2,1)}, bf16[1024,384]{1,0:T(8,128)(2,1)}, u32[]{:S(2)}, u32[]{:S(2)}) collective-permute-start(bf16[1024,384]{1,0:T(8,128)(2,1)} %bitcast.77), channel_id=1, source_target_pairs={{0,24},{8,32},{16,40},{24,48},{32,56},{40,64},{48,72},{56,80},{64,... | collective-permute-start | bytes 2359304 | tf_op jit(solution)/shard_map/ppermute | solution.py:13
  97.3 71.8 %collective-permute-start.3 = (bf16[1024,384]{1,0:T(8,128)(2,1)}, bf16[1024,384]{1,0:T(8,128)(2,1)}, u32[]{:S(2)}, u32[]{:S(2)}) collective-permute-start(bf16[1024,384]{1,0:T(8,128)(2,1)} %bitcast.78), channel_id=1, source_target_pairs={{0,32},{8,40},{16,48},{24,56},{32,64},{40,72},{48,80},{56,88},{64,... | collective-permute-start | bytes 2359304 | tf_op jit(solution)/shard_map/ppermute | solution.py:13
  110.1 3.0 %copy-start.1 = (bf16[1024,384]{0,1:T(8,128)(2,1)S(1)}, bf16[1024,384]{0,1:T(8,128)(2,1)}, u32[]{:S(2)}) copy-start(bf16[1024,384]{0,1:T(8,128)(2,1)} %copy.57) | copy-start | bytes 2359300
  171.5 6.3 %copy-start.3 = (bf16[2,512,3,128]{1,0,3,2:T(2,128)(2,1)S(1)}, bf16[2,512,3,128]{1,0,3,2:T(2,128)(2,1)}, u32[]{:S(2)}) copy-start(bf16[2,512,3,128]{1,0,3,2:T(2,128)(2,1)} %custom-call.3) | copy-start | bytes 2359300
  177.8 101.4 %copy-start.5 = (pred[8,128]{1,0:T(8,128)(4,1)S(1)}, pred[8,128]{1,0:T(8,128)(4,1)}, u32[]{:S(2)}) copy-start(pred[8,128]{1,0:T(8,128)(4,1)} %add_compare_fusion) | copy-start | bytes 3076
  192.5 14.3 %copy-start = (bf16[5120,3,128]{2,0,1:T(8,128)(2,1)S(1)}, bf16[5120,3,128]{2,0,1:T(8,128)(2,1)}, u32[]{:S(2)}) copy-start(bf16[5120,3,128]{2,0,1:T(8,128)(2,1)} %get-tuple-element.137) | copy-start | bytes 11796484 | tf_op jit(solution)/shard_map/while
  242.9 14.3 %copy-start = (bf16[5120,3,128]{2,0,1:T(8,128)(2,1)S(1)}, bf16[5120,3,128]{2,0,1:T(8,128)(2,1)}, u32[]{:S(2)}) copy-start(bf16[5120,3,128]{2,0,1:T(8,128)(2,1)} %get-tuple-element.137) | copy-start | bytes 11796484 | tf_op jit(solution)/shard_map/while
where the time goes:
time: 296 us; the launch traced here: 294 us
  waiting for transfers between devices  81.1 us (27%)
  local copies, waits for them, and re-layouts  64.5 us (22%)
  matrix products  56.9 us (19%)
  starting transfers between devices  44 us (15%)
  other arithmetic  33.2 us (11%)
  blocking collectives  13.8 us (5%)
    ppermute x8, waiting for transfers between devices, from_behind(): return lax.ppermute(block, axis, route)  47.8 us
    ppermute x8, starting transfers between devices, from_behind(): return lax.ppermute(block, axis, route)  30.8 us
    dot_general x2, matrix products, attend(): jnp.einsum('qhd,khd->hqk', query_block, key_all, preferred_element_type=j...  29.3 us
    reduce_sum x2, other arithmetic, attend(): total = jnp.sum(weights, axis=2)  28.6 us
    dot_general x2, matrix products, attend(): jnp.einsum('hqk,khd->qhd', rounded, value_all, preferred_element_type=jnp...  27.6 us
    all_to_all x1, waiting for transfers between devices, on_device(): lax.all_to_all(keys, 'head', split_axis=1, concat_axis=0, tiled=True)  24.3 us
    dynamic_update_slice x4, local copies, waits for them, and re-layouts, on_device(): lax.map(attend, query_blocks).reshape(stretch_rows, head_count, HEAD_DIM)  15.3 us
    all_to_all x1, blocking collectives, on_device(): lax.all_to_all(outgoing, 'head', split_axis=0, concat_axis=1, tiled=True)  13.8 us
  transfers between devices with their start and end apart: 11, of which 7 were waited for; matrix products, arithmetic and copies ran while one was open for 14% of the time, Pallas kernels for 0%

commit v1 on v0

v1 whole, which is shorter than its diff:
```python
import functools
import math

import jax
import jax.numpy as jnp
from jax import lax
from jax.experimental import pallas as pl
from jax.experimental.pallas import tpu as pltpu
from jax.sharding import Mesh
from jax.sharding import PartitionSpec as P

HEAD_DIM = 128
ROWS = 128
GROUPS = 8
HALF = ROWS // 2
CHUNK = ROWS // 4
PLANE = 4
STRETCH = GROUPS * ROWS
QUERIES = STRETCH + STRETCH // 2
TILE = 512
TILES = QUERIES // TILE
OWN_TILES = STRETCH // TILE
STEP = 256
Q_ROWS = ROWS + HALF
KV_ROWS = 2 * ROWS
PAYLOAD = Q_ROWS + 2 * KV_ROWS
BACK_ROWS = KV_ROWS + ROWS
SCALE = HEAD_DIM**-0.5 * math.log2(math.e)
LOWEST = -1e30
AXES = ("z", "xh", "core", "head")
BIG, MIDDLE, SMALL = (pltpu.CompilerParams(vmem_limit_bytes=n * 2**20) for n in (62, 36, 4))
SMEM = pl.BlockSpec(memory_space=pltpu.SMEM)
WHOLE = pl.BlockSpec(memory_space=pltpu.VMEM)
ANY = pl.BlockSpec(memory_space=pl.ANY)
HBM = pl.BlockSpec(memory_space=pltpu.HBM)


def first_pack_body(q_ref, k_ref, v_ref, out_ref, mid_ref, wide, slots, in_sem, out_sem, mid_sem):
    loads = start(
        [
            pltpu.make_async_copy(ref, wide.at[n], in_sem.at[n])
            for n, ref in enumerate((k_ref, q_ref, v_ref))
        ]
    )
    loads[0].wait()
    stores = start(
        [
            pltpu.make_async_copy(wide.at[0, :, middle(g)], mid_ref.at[g], mid_sem.at[g])
            for g in range(GROUPS)
        ]
    )
    wait(loads[1:])
    for g in range(GROUPS):
        for half in range(2):
            own = slice((3 * g + 2 * half) * HEAD_DIM, (3 * g + 2 * half + 1) * HEAD_DIM)
            slots[half, g, 0:ROWS] = wide[1, :, own]
            slots[half, g, ROWS:Q_ROWS] = wide[1, half * HALF : (half + 1) * HALF, middle(g)]
            for n, at in ((0, Q_ROWS), (2, Q_ROWS + KV_ROWS)):
                slots[half, g, at : at + ROWS] = wide[n, :, own]
                slots[half, g, at + ROWS : at + KV_ROWS] = wide[n, :, middle(g)]
            stores += store_slot(slots, out_ref, out_sem, half, g)
    wait(stores)


def back_pack_body(v_ref, mid_ref, out_ref, wide, slots, in_sem, out_sem, mid_sem):
    load = start([pltpu.make_async_copy(v_ref, wide.at[0], in_sem.at[0])])
    mids = start(
        [
            pltpu.make_async_copy(
                mid_ref, slots.at[half, :, KV_ROWS:BACK_ROWS], mid_sem.at[half]
            )
            for half in range(2)
        ]
    )
    wait(load + mids)
    stores = []
    for g in range(GROUPS):
        for half in range(2):
            own = slice((3 * g + 2 * half) * HEAD_DIM, (3 * g + 2 * half + 1) * HEAD_DIM)
            slots[half, g, 0:ROWS] = wide[0, :, own]
            slots[half, g, ROWS:KV_ROWS] = wide[0, :, middle(g)]
            stores += store_slot(slots, out_ref, out_sem, half, g)
    wait(stores)


def middle(g):
    return slice((3 * g + 1) * HEAD_DIM, (3 * g + 2) * HEAD_DIM)


def store_slot(slots, out_ref, out_sem, half, g):
    copy = pltpu.make_async_copy(slots.at[half, g], out_ref.at[half, g], out_sem.at[half, g])
    return start([copy])


def pack(body, rows, also, *arrays):
    slots = jax.ShapeDtypeStruct((2, GROUPS, rows, HEAD_DIM), jnp.bfloat16)
    middles = jax.ShapeDtypeStruct((GROUPS, ROWS, HEAD_DIM), jnp.bfloat16)
    return pl.pallas_call(
        body,
        in_specs=[HBM] * len(arrays),
        out_specs=[HBM] * (1 + also),
        out_shape=[slots, middles][: 1 + also],
        scratch_shapes=[
            pltpu.VMEM((3 if also else 1, ROWS, GROUPS * 3 * HEAD_DIM), jnp.bfloat16),
            pltpu.VMEM(slots.shape, slots.dtype),
            pltpu.SemaphoreType.DMA((3,)),
            pltpu.SemaphoreType.DMA((2, GROUPS)),
            pltpu.SemaphoreType.DMA((GROUPS,)),
        ],
        compiler_params=BIG,
    )(*arrays)


def unpack_body(in_ref, out_ref, wide, sem):
    stores = []
    for n in range(ROWS // CHUNK):
        rows = slice(n * CHUNK, (n + 1) * CHUNK)
        half, first = divmod(n * CHUNK, HALF)
        for g in range(GROUPS):
            for k in range(2):
                own = slice((3 * g + 2 * k) * HEAD_DIM, (3 * g + 2 * k + 1) * HEAD_DIM)
                wide[rows, own] = in_ref[k, g, rows]
            wide[rows, middle(g)] = in_ref[half, g, ROWS + first : ROWS + first + CHUNK]
        stores += start([pltpu.make_async_copy(wide.at[rows], out_ref.at[rows], sem.at[n])])
    wait(stores)


def unpack(array):
    wide = jax.ShapeDtypeStruct((ROWS, GROUPS * 3 * HEAD_DIM), jnp.bfloat16)
    return pl.pallas_call(
        unpack_body,
        in_specs=[WHOLE],
        out_specs=ANY,
        out_shape=wide,
        scratch_shapes=[
            pltpu.VMEM(wide.shape, wide.dtype), pltpu.SemaphoreType.DMA((ROWS // CHUNK,))
        ],
        compiler_params=SMALL,
    )(array)


def fold(slot, q_own, q_shared, acc_ref, top_ref, own, shared, count, limit):
    def score(tile):
        blocks = slice(tile * TILE // ROWS, (tile + 1) * TILE // ROWS)
        queries = q_own[slot, blocks] if tile < OWN_TILES else q_shared[slot]
        return lax.dot_general(
            queries.reshape(TILE, HEAD_DIM),
            (own if tile < OWN_TILES else shared)[0],
            (((1,), (1,)), ((), ())),
            preferred_element_type=jnp.float32,
        )

    def weigh(tile, scores):
        if limit is not None:
            head, tail = scores[:, : count - STEP], scores[:, count - STEP :]
            column = lax.broadcasted_iota(jnp.int32, tail.shape, 1)
            tail = jnp.where(column < limit - (count - STEP), tail, LOWEST)
            scores = jnp.concatenate([head, tail], 1)
        old = top_ref[slot, tile * TILE : (tile + 1) * TILE]
        new = jnp.maximum(old, jnp.max(scores, axis=1, keepdims=True) * SCALE)
        weights = jnp.exp2(scores * SCALE - jnp.concatenate([new] * (count // HEAD_DIM), 1))
        return weights.astype(jnp.bfloat16), jnp.exp2(old - new), new

    def mix(tile, weights, decay, new):
        rows = slice(tile * TILE, (tile + 1) * TILE)
        values = (own if tile < OWN_TILES else shared)[1]
        wide = jnp.concatenate([values, jnp.ones_like(values)], 1)
        mixed = jnp.dot(weights, wide, preferred_element_type=jnp.float32)
        acc_ref[slot, rows] = acc_ref[slot, rows] * jnp.concatenate([decay, decay], 1) + mixed
        top_ref[slot, rows] = new

    scores = score(0)
    for tile in range(TILES):
        ahead = score(tile + 1) if tile + 1 < TILES else None
        mix(tile, *weigh(tile, scores))
        scores = ahead


def sweep(earlier, visible_ref, lengths_ref, queries, acc_ref, top_ref, places, arrived):
    z, core = lax.axis_index("z"), lax.axis_index("core")
    acc_ref[...] = jnp.zeros_like(acc_ref)
    top_ref[...] = jnp.full_like(top_ref, LOWEST)
    for other in range(2):
        arrived(other)

        def step(n, carry):
            slot, x = n // 2, n % 2
            stretch = PLANE * z + 2 * slot + core
            reach = jnp.minimum(visible_ref[stretch], stretch)
            back = earlier * PLANE + 2 * (slot - x) + other * (2 * core - 1)
            seen = jnp.logical_and(back >= 0, back <= reach)
            length = lengths_ref[jnp.maximum(stretch - back, 0)]
            for count in range(STRETCH // 2, STRETCH + 1, STEP):
                fits = length <= count
                if count > STRETCH // 2:
                    fits = jnp.logical_and(fits, length > count - STEP)

                @pl.when(jnp.logical_and(seen, fits))
                def _():
                    def part(scr, at):
                        rows = scr[other, x, 0 : count // ROWS, at : at + ROWS]
                        return rows.reshape(count, HEAD_DIM)

                    parts = [part(*place) for place in places]
                    limit = None if count == STRETCH // 2 else length
                    fold(slot, *queries, acc_ref, top_ref, parts[:2], parts[2:], count, limit)

            return carry

        lax.fori_loop(0, 4, step, 0)


def start(copies):
    for copy in copies:
        copy.start()
    return copies


def wait(copies):
    for copy in copies:
        copy.wait()


def load_queries(here_ref, q_own, q_shared, sem):
    return start(
        [
            pltpu.make_async_copy(here_ref.at[:, :, 0:ROWS], q_own, sem.at[0]),
            pltpu.make_async_copy(here_ref.at[:, :, ROWS:Q_ROWS], q_shared, sem.at[1]),
        ]
    )


def own_body(
    visible_ref, lengths_ref, here_ref, mate_ref,
    mixed_ref, level_ref, acc_ref, top_ref, q_own, q_shared, q_sem, kv_scr, kv_sem,
):
    loads = load_queries(here_ref, q_own, q_shared, q_sem)
    loads += start(
        [
            pltpu.make_async_copy(ref.at[:, :, Q_ROWS:], kv_scr.at[n], kv_sem.at[n])
            for n, ref in enumerate((here_ref, mate_ref))
        ]
    )
    sweep(
        0, visible_ref, lengths_ref, (q_own, q_shared), acc_ref, top_ref,
        [(kv_scr, at) for at in (0, KV_ROWS, ROWS, KV_ROWS + ROWS)],
        lambda other: wait(loads[3:] if other else loads[:3]),
    )
    total = acc_ref[:, :, HEAD_DIM:]
    mixed_ref[...] = acc_ref[:, :, 0:HEAD_DIM] / total
    level_ref[...] = top_ref[...] + jnp.log2(total)


def earlier_body(
    visible_ref, lengths_ref, here_ref, k_back, k_mate, v_back, v_mate, mixed_in, level_in,
    out_ref, mixed_own, level_own, acc_ref, top_ref, q_own, q_shared, q_sem, k_scr, v_scr, kv_sem,
    own_sem,
):
    loads = load_queries(here_ref, q_own, q_shared, q_sem)
    loads += start(
        [
            pltpu.make_async_copy(ref, scr.at[n], kv_sem.at[n, m])
            for n, pair in enumerate(((k_back, v_back), (k_mate, v_mate)))
            for m, (ref, scr) in enumerate(zip(pair, (k_scr, v_scr)))
        ]
    )
    state = start(
        [
            pltpu.make_async_copy(mixed_in, mixed_own, own_sem.at[0]),
            pltpu.make_async_copy(level_in, level_own, own_sem.at[1]),
        ]
    )
    sweep(
        1, visible_ref, lengths_ref, (q_own, q_shared), acc_ref, top_ref,
        [(k_scr, 0), (v_scr, 0), (v_scr, KV_ROWS), (v_scr, ROWS)],
        lambda other: wait(loads[4:] if other else loads[:4]),
    )
    wait(state)
    z, xh, core = (lax.axis_index(name) for name in ("z", "xh", "core"))

    def token(count, step, first):
        row = lax.broadcasted_iota(jnp.int32, (count, HEAD_DIM), 0)
        return (row // step) * ROWS + first + row % step

    for slot in range(2):
        length = lengths_ref[PLANE * z + 2 * slot + core]
        for rows, tokens, height, at in (
            (slice(0, STRETCH), token(STRETCH, ROWS, 0), ROWS, 0),
            (slice(STRETCH, QUERIES), token(STRETCH // 2, HALF, xh * HALF), HALF, ROWS),
        ):
            top = jnp.maximum(top_ref[slot, rows], level_own[slot, rows])
            now, before = jnp.exp2(level_own[slot, rows] - top), jnp.exp2(top_ref[slot, rows] - top)
            mixed = mixed_own[slot, rows] * now + acc_ref[slot, rows, 0:HEAD_DIM] * before
            total = now + acc_ref[slot, rows, HEAD_DIM:] * before
            mixed = jnp.where(tokens < length, mixed / total, 0.0).astype(jnp.bfloat16)
            out_ref[slot, :, at : at + height] = mixed.reshape(GROUPS, height, HEAD_DIM)


STATE = [jax.ShapeDtypeStruct((2, QUERIES, HEAD_DIM), jnp.float32)] * 2
STATE_SCRATCH = [pltpu.VMEM((2, QUERIES, width), jnp.float32) for width in (2 * HEAD_DIM, HEAD_DIM)]
LOAD_SCRATCH = [
    pltpu.VMEM((2, GROUPS, ROWS, HEAD_DIM), jnp.bfloat16),
    pltpu.VMEM((2, GROUPS, HALF, HEAD_DIM), jnp.bfloat16),
    pltpu.SemaphoreType.DMA((2,)),
]


def key_scratch(rows):
    return pltpu.VMEM((2, 2, GROUPS, rows, HEAD_DIM), jnp.bfloat16)


COST = pl.CostEstimate(flops=10**9, bytes_accessed=10**6, transcendentals=10**6)


def attend_own(visible, lengths, here, mate):
    return pl.pallas_call(
        own_body,
        in_specs=[SMEM, SMEM, ANY, ANY],
        out_specs=[WHOLE] * 2,
        out_shape=STATE,
        scratch_shapes=STATE_SCRATCH
        + LOAD_SCRATCH
        + [key_scratch(2 * KV_ROWS), pltpu.SemaphoreType.DMA((2,))],
        compiler_params=MIDDLE,
        cost_estimate=COST,
    )(visible, lengths, here, mate)


def attend_earlier(visible, lengths, here, k_back, k_mate, v_back, v_mate, mixed, level):
    return pl.pallas_call(
        earlier_body,
        in_specs=[SMEM, SMEM] + [ANY] * 7,
        out_specs=WHOLE,
        out_shape=jax.ShapeDtypeStruct((2, GROUPS, Q_ROWS, HEAD_DIM), jnp.bfloat16),
        scratch_shapes=[pltpu.VMEM(s.shape, s.dtype) for s in STATE]
        + STATE_SCRATCH
        + LOAD_SCRATCH
        + [key_scratch(ROWS), key_scratch(BACK_ROWS)]
        + [pltpu.SemaphoreType.DMA((2, 2)), pltpu.SemaphoreType.DMA((2,))],
        compiler_params=MIDDLE,
        cost_estimate=COST,
    )(visible, lengths, here, k_back, k_mate, v_back, v_mate, mixed, level)


def tie_body(*refs):
    pass


def tie(after, *arrays):
    return pl.pallas_call(
        tie_body,
        in_specs=[ANY] * (len(arrays) + 1),
        out_specs=[ANY] * len(arrays),
        out_shape=[jax.ShapeDtypeStruct(array.shape, array.dtype) for array in arrays],
        input_output_aliases={n: n for n in range(len(arrays))},
        compiler_params=SMALL,
    )(*arrays, after)


def split_body(here_ref, _, out_ref, keys_ref, scr, in_sem, out_sem):
    def load(half):
        part = here_ref.at[half, :, Q_ROWS : Q_ROWS + ROWS]
        return pltpu.make_async_copy(part, scr.at[half], in_sem.at[half])

    loads = start([load(half) for half in range(2)])
    stores = []
    for half in range(2):
        loads[half].wait()
        stores += start(
            [pltpu.make_async_copy(scr.at[half], keys_ref.at[half], out_sem.at[half])]
        )
    wait(stores)


def split_keys(here, after):
    keys = jax.ShapeDtypeStruct((2, GROUPS, ROWS, HEAD_DIM), here.dtype)
    return pl.pallas_call(
        split_body,
        in_specs=[HBM, HBM],
        out_specs=[HBM, HBM],
        out_shape=[jax.ShapeDtypeStruct(here.shape, here.dtype), keys],
        input_output_aliases={0: 0},
        scratch_shapes=[pltpu.VMEM(keys.shape, keys.dtype)] + [pltpu.SemaphoreType.DMA((2,))] * 2,
        compiler_params=BIG,
    )(here, after)


def exchange(array):
    flat = array.reshape((2 * GROUPS,) + array.shape[2:])
    flat = lax.all_to_all(flat, ("xh", "head"), 0, 0)
    return flat.reshape(array.shape)


def to_next_plane(array):
    planes = lax.axis_size("z")
    return lax.ppermute(array, "z", [(i, i + 1) for i in range(planes - 1)])


def to_other_core(array):
    return lax.ppermute(array, "core", [(0, 1), (1, 0)])


def on_device(queries, keys, values, visible, lengths):
    v_raw = to_next_plane(values)
    packed, k_middle = pack(first_pack_body, PAYLOAD, True, queries, keys, values)
    here = exchange(packed)
    (packed,) = pack(back_pack_body, BACK_ROWS, False, v_raw, to_next_plane(k_middle))
    (here,) = tie(packed, here)
    mate = to_other_core(here)
    here, k_here = split_keys(here, mate)
    k_back, v_back = to_next_plane(k_here), exchange(packed)
    mixed, level = attend_own(visible, lengths, here, mate)
    k_back, v_back = tie(mixed, k_back, v_back)
    out = attend_earlier(
        visible, lengths, here, k_back, to_other_core(k_back), v_back, to_other_core(v_back),
        mixed, level,
    )
    return unpack(exchange(out))


def solution(mesh):
    planes = mesh.devices.shape[0] // PLANE
    fine = Mesh(mesh.devices.reshape(planes, 2, 2, GROUPS), AXES)
    rows = P(AXES, None)
    return jax.shard_map(
        on_device,
        mesh=fine,
        in_specs=(rows, rows, rows, P(), P()),
        out_specs=rows,
        check_vma=False,
    )
```

time: 296 us -> 118 us (0.40)
  the two profiles are of different devices: /device:TPU:69 before, /device:TPU:64 now
where the time goes in v1:
time: 118 us; the launch traced here: 116 us
  waiting for transfers between devices  37.2 us (32%)
  Pallas kernels  31.3 us (27%)
  starting transfers between devices  26.7 us (23%)
  blocking collectives  14.7 us (12%)
  local copies, waits for them, and re-layouts  5.3 us (4%)
    ppermute x3, waiting for transfers between devices, to_next_plane(): return lax.ppermute(array, 'z', [(i, i + 1) for i in range(planes - 1)])  17.6 us
    all_to_all x2, waiting for transfers between devices, exchange(): flat = lax.all_to_all(flat, ('xh', 'head'), 0, 0)  15.9 us
    all_to_all x1, blocking collectives, exchange(): flat = lax.all_to_all(flat, ('xh', 'head'), 0, 0)  14.7 us
    all_to_all x2, starting transfers between devices, exchange(): flat = lax.all_to_all(flat, ('xh', 'head'), 0, 0)  13.4 us
    ppermute x3, starting transfers between devices, to_next_plane(): return lax.ppermute(array, 'z', [(i, i + 1) for i in range(planes - 1)])  12.9 us
    pallas_call x1, Pallas kernels, attend_earlier(): pl.pallas_call(earlier_body, in_specs=[SMEM, SMEM] + [ANY] * 7, out_specs...  12.2 us
    pallas_call x1, Pallas kernels, attend_own(): pl.pallas_call(own_body, in_specs=[SMEM, SMEM, ANY, ANY], out_specs=[WHOL...  10.3 us
    pallas_call x2, Pallas kernels, pack(): pl.pallas_call(body, in_specs=[HBM] * len(arrays), out_specs=[HBM] * (1 +...  6.1 us
  transfers between devices with their start and end apart: 8, of which 4 were waited for; matrix products, arithmetic and copies ran while one was open for 0% of the time, Pallas kernels for 13%

profile of v1, /device:TPU:64, one launch (start us, length us, event | category | flops | bytes accessed | tf_op | source)
XLA Modules:
  0.0 115.5 jit_solution(4859867820407487149)
XLA Ops:
  0.0 3.4 %shard_map.55 = (bf16[2,8,704,128]{3,2,1,0:T(8,128)(2,1)}, bf16[8,128,128]{2,1,0:T(8,128)(2,1)}) custom-call(bf16[128,3072]{1,0:T(8,128)(2,1)} %q_ref.1, bf16[128,3072]{1,0:T(8,128)(2,1)} %k_ref.1, bf16[128,3072]{1,0:T(8,128)(2,1)} %v_ref.1), custom_call_target="tpu_custom_call" | custom-call | tf_op jit(solution)/shard_map/pallas_call | solution.py:98
  3.4 0.0 copy-start.7
  3.5 0.0 copy-start.10
  3.5 7.2 %all-to-all-start = ((bf16[16,704,128]{2,1,0:T(8,128)(2,1)}), bf16[16,704,128]{2,1,0:T(8,128)(2,1)}, u32[]{:S(2)}, u32[]{:S(2)}) async-start(bf16[16,704,128]{2,1,0:T(8,128)(2,1)} %bitcast.9), calls=%async_computation | async-start | bytes 5767168 | tf_op jit(solution)/shard_map/all_to_all | solution.py:390
  10.7 3.8 %collective-permute-start = (bf16[128,3072]{1,0:T(8,128)(2,1)S(1)}, bf16[128,3072]{1,0:T(8,128)(2,1)S(1)}, u32[]{:S(2)}, u32[]{:S(2)}) collective-permute-start(bf16[128,3072]{1,0:T(8,128)(2,1)S(1)} %copy-done.7), channel_id=1, source_target_pairs={{0,32},{32,64},{64,96},{96,128},{128,160},{160,192},{192,224},{1,3... | collective-permute-start | bytes 2359304 | tf_op jit(solution)/shard_map/ppermute | solution.py:396
  14.6 5.0 %collective-permute-start.1 = (bf16[8,128,128]{2,1,0:T(8,128)(2,1)S(1)}, bf16[8,128,128]{2,1,0:T(8,128)(2,1)S(1)}, u32[]{:S(2)}, u32[]{:S(2)}) collective-permute-start(bf16[8,128,128]{2,1,0:T(8,128)(2,1)S(1)} %copy-done.10), channel_id=1, source_target_pairs={{0,32},{32,64},{64,96},{96,128},{128,160},{160,192},{192,224},{1,3... | collective-permute-start | bytes 786440 | tf_op jit(solution)/shard_map/ppermute | solution.py:396
  19.6 17.6 %collective-permute-done.1.mid_ref = bf16[8,128,128]{2,1,0:T(8,128)(2,1)S(1)} collective-permute-done((bf16[8,128,128]{2,1,0:T(8,128)(2,1)S(1)}, bf16[8,128,128]{2,1,0:T(8,128)(2,1)S(1)}, u32[]{:S(2)}, u32[]{:S(2)}) %collective-permute-start.1) | collective-permute-done | bytes 262176 | tf_op jit(solution)/shard_map/ppermute | solution.py:396
  37.2 0.0 collective-permute-done.v_ref
  37.2 0.7 copy-done.9
  37.9 0.9 copy-done.8
  38.8 2.7 %shard_map.56.refs_1_ = bf16[2,8,384,128]{3,2,1,0:T(8,128)(2,1)} custom-call(bf16[128,3072]{1,0:T(8,128)(2,1)} %copy-done.8, bf16[8,128,128]{2,1,0:T(8,128)(2,1)} %copy-done.9), custom_call_target="tpu_custom_call" | custom-call | tf_op jit(solution)/shard_map/pallas_call | solution.py:98
  41.5 9.0 %all-to-all-done = bf16[16,704,128]{2,1,0:T(8,128)(2,1)} async-done(((bf16[16,704,128]{2,1,0:T(8,128)(2,1)}), bf16[16,704,128]{2,1,0:T(8,128)(2,1)}, u32[]{:S(2)}, u32[]{:S(2)}) %all-to-all-start) | async-done | bytes 2883616 | tf_op jit(solution)/shard_map/all_to_all | solution.py:390
  50.5 0.0 collective-permute-start.2
  50.5 6.1 %all-to-all-start.1 = ((bf16[16,384,128]{2,1,0:T(8,128)(2,1)}), bf16[16,384,128]{2,1,0:T(8,128)(2,1)S(1)}, u32[]{:S(2)}, u32[]{:S(2)}) async-start(bf16[16,384,128]{2,1,0:T(8,128)(2,1)} %bitcast.2), calls=%async_computation.1 | async-start | bytes 3145728 | tf_op jit(solution)/shard_map/all_to_all | solution.py:390
  56.6 0.0 copy-start.5
  56.6 0.0 copy-start.6
  56.6 0.0 collective-permute-done.2._.mate_ref
  56.7 1.8 %shard_map.58 = (bf16[2,8,704,128]{3,2,1,0:T(8,128)(2,1)}, bf16[2,8,128,128]{3,2,1,0:T(8,128)(2,1)}) custom-call(bf16[2,8,704,128]{3,2,1,0:T(8,128)(2,1)} %shard_map.57.here_ref, bf16[2,8,704,128]{3,2,1,0:T(8,128)(2,1)} %collective-permute-done.2._.mate_ref), custom_call_target="tpu_custom_call", output_to_operand_aliasing={{0}: (0, {})} | custom-call | tf_op jit(solution)/shard_map/pallas_call | solution.py:377
  58.4 4.0 %collective-permute-start.3 = (bf16[2,8,128,128]{3,2,1,0:T(8,128)(2,1)}, bf16[2,8,128,128]{3,2,1,0:T(8,128)(2,1)S(1)}, u32[]{:S(2)}, u32[]{:S(2)}) collective-permute-start(bf16[2,8,128,128]{3,2,1,0:T(8,128)(2,1)} %get-tuple-element.16), channel_id=1, source_target_pairs={{0,32},{32,64},{64,96},{96,128},{128,160},{160,192},{192,224},{1,3... | collective-permute-start | bytes 1572872 | tf_op jit(solution)/shard_map/ppermute | solution.py:396
  62.5 10.3 %shard_map.59 = (f32[2,1536,128]{2,1,0:T(8,128)S(1)}, f32[2,1536,128]{2,1,0:T(8,128)S(1)}) custom-call(s32[32]{0:T(128)S(1)} %copy-done.5, s32[32]{0:T(128)S(1)} %copy-done.6, bf16[2,8,704,128]{3,2,1,0:T(8,128)(2,1)} %get-tuple-element.15.here_ref, bf16[2,8,704,128]{3,2,1,0:T(8,128)(2,1)} %collective-permute-done.2._.mate_ref), custom_call_target="tpu_custom_call" | custom-call | flops 1000000000 | bytes 1000000 | tf_op jit(solution)/shard_map/pallas_call | solution.py:316
  72.8 1.2 %copy-done = f32[2,1536,128]{2,1,0:T(8,128)} copy-done((f32[2,1536,128]{2,1,0:T(8,128)}, f32[2,1536,128]{2,1,0:T(8,128)S(1)}, u32[]{:S(2)}) %copy-start) | copy-done | bytes 1572888
  73.9 1.1 copy-done.3
  75.1 6.9 %all-to-all-done.1 = bf16[16,384,128]{2,1,0:T(8,128)(2,1)S(1)} async-done(((bf16[16,384,128]{2,1,0:T(8,128)(2,1)}), bf16[16,384,128]{2,1,0:T(8,128)(2,1)S(1)}, u32[]{:S(2)}, u32[]{:S(2)}) %all-to-all-start.1) | async-done | bytes 1572896 | tf_op jit(solution)/shard_map/all_to_all | solution.py:390
  81.9 0.0 collective-permute-done.3.refs_0_
  81.9 1.4 %copy-done.1 = f32[2,1536,128]{2,1,0:T(8,128)S(1)} copy-done((f32[2,1536,128]{2,1,0:T(8,128)S(1)}, f32[2,1536,128]{2,1,0:T(8,128)}, u32[]{:S(2)}) %copy-start.1) | copy-done | bytes 1572888
  83.4 0.0 collective-permute-start.5
  83.4 0.5 collective-permute-start.4
  83.9 3.6 %collective-permute-done.4.k_mate = bf16[2,8,128,128]{3,2,1,0:T(8,128)(2,1)S(1)} collective-permute-done((bf16[2,8,128,128]{3,2,1,0:T(8,128)(2,1)S(1)}, bf16[2,8,128,128]{3,2,1,0:T(8,128)(2,1)S(1)}, u32[]{:S(2)}, u32[]{:S(2)}) %collective-permute-start.4) | collective-permute-done | bytes 524320 | tf_op jit(solution)/shard_map/ppermute | solution.py:400
  87.5 0.0 collective-permute-done.5.v_mate
  87.5 12.2 %shard_map.61 = bf16[2,8,192,128]{3,2,1,0:T(8,128)(2,1)S(1)} custom-call(s32[32]{0:T(128)S(1)} %copy-done.5, s32[32]{0:T(128)S(1)} %copy-done.6, bf16[2,8,704,128]{3,2,1,0:T(8,128)(2,1)} %get-tuple-element.15.here_ref, bf16[2,8,128,128]{3,2,1,0:T(8,128)(2,1)S(1)} %get-tuple-element.18.k_back, bf16[2,8,128,128]{3,2,1,0:T(8,128)(2,1)S(1)} %collective-permute-done.4.k_mate, ...), custom_call_target="tpu_custom_call" | custom-call | flops 1000000000 | bytes 1000000 | tf_op jit(solution)/shard_map/pallas_call | solution.py:330
  99.7 14.7 %all_to_all.15 = bf16[16,192,128]{2,1,0:T(8,128)(2,1)S(1)} all-to-all(bf16[16,192,128]{2,1,0:T(8,128)(2,1)S(1)} %bitcast.7), channel_id=1, replica_groups=mesh['z'=8,'xh'=2,'core'=2,'head'=8] {'xh','head'}, dimensions={0} | all-to-all | bytes 1572864 | tf_op jit(solution)/shard_map/all_to_all | solution.py:390
  114.4 0.9 shard_map.62
  (15 shorter events, 0.0 us)
Async XLA Ops:
  3.4 7.3 %copy-start.7 = (bf16[128,3072]{1,0:T(8,128)(2,1)S(1)}, bf16[128,3072]{1,0:T(8,128)(2,1)}, u32[]{:S(2)}) copy-start(bf16[128,3072]{1,0:T(8,128)(2,1)} %v_ref.1) | copy-start | bytes 2359300
  3.5 11.1 %copy-start.10 = (bf16[8,128,128]{2,1,0:T(8,128)(2,1)S(1)}, bf16[8,128,128]{2,1,0:T(8,128)(2,1)}, u32[]{:S(2)}) copy-start(bf16[8,128,128]{2,1,0:T(8,128)(2,1)} %get-tuple-element.14) | copy-start | bytes 786436
  3.5 47.0 %all-to-all-start = ((bf16[16,704,128]{2,1,0:T(8,128)(2,1)}), bf16[16,704,128]{2,1,0:T(8,128)(2,1)}, u32[]{:S(2)}, u32[]{:S(2)}) async-start(bf16[16,704,128]{2,1,0:T(8,128)(2,1)} %bitcast.9), calls=%async_computation | async-start | bytes 5767168 | tf_op jit(solution)/shard_map/all_to_all | solution.py:390
  10.7 26.5 %collective-permute-start = (bf16[128,3072]{1,0:T(8,128)(2,1)S(1)}, bf16[128,3072]{1,0:T(8,128)(2,1)S(1)}, u32[]{:S(2)}, u32[]{:S(2)}) collective-permute-start(bf16[128,3072]{1,0:T(8,128)(2,1)S(1)} %copy-done.7), channel_id=1, source_target_pairs={{0,32},{32,64},{64,96},{96,128},{128,160},{160,192},{192,224},{1,3... | collective-permute-start | bytes 2359304 | tf_op jit(solution)/shard_map/ppermute | solution.py:396
  14.6 22.7 %collective-permute-start.1 = (bf16[8,128,128]{2,1,0:T(8,128)(2,1)S(1)}, bf16[8,128,128]{2,1,0:T(8,128)(2,1)S(1)}, u32[]{:S(2)}, u32[]{:S(2)}) collective-permute-start(bf16[8,128,128]{2,1,0:T(8,128)(2,1)S(1)} %copy-done.10), channel_id=1, source_target_pairs={{0,32},{32,64},{64,96},{96,128},{128,160},{160,192},{192,224},{1,3... | collective-permute-start | bytes 786440 | tf_op jit(solution)/shard_map/ppermute | solution.py:396
  37.2 0.7 copy-start.9
  37.9 0.9 copy-start.8
  50.5 6.2 %collective-permute-start.2 = (bf16[2,8,704,128]{3,2,1,0:T(8,128)(2,1)}, bf16[2,8,704,128]{3,2,1,0:T(8,128)(2,1)}, u32[]{:S(2)}, u32[]{:S(2)}) collective-permute-start(bf16[2,8,704,128]{3,2,1,0:T(8,128)(2,1)} %shard_map.57.here_ref), channel_id=1, source_target_pairs={{0,8},{8,0},{1,9},{9,1},{2,10},{10,2},{3,11},{11,3},{4,12},{12,4},... | collective-permute-start | bytes 8650760 | tf_op jit(solution)/shard_map/ppermute | solution.py:400
  50.5 31.5 %all-to-all-start.1 = ((bf16[16,384,128]{2,1,0:T(8,128)(2,1)}), bf16[16,384,128]{2,1,0:T(8,128)(2,1)S(1)}, u32[]{:S(2)}, u32[]{:S(2)}) async-start(bf16[16,384,128]{2,1,0:T(8,128)(2,1)} %bitcast.2), calls=%async_computation.1 | async-start | bytes 3145728 | tf_op jit(solution)/shard_map/all_to_all | solution.py:390
  56.6 5.8 %copy-start.5 = (s32[32]{0:T(128)S(1)}, s32[32]{0:T(128)}, u32[]{:S(2)}) copy-start(s32[32]{0:T(128)} %visible_ref.3) | copy-start | bytes 388
  56.6 5.8 %copy-start.6 = (s32[32]{0:T(128)S(1)}, s32[32]{0:T(128)}, u32[]{:S(2)}) copy-start(s32[32]{0:T(128)} %lengths_ref.3) | copy-start | bytes 388
  58.4 23.5 %collective-permute-start.3 = (bf16[2,8,128,128]{3,2,1,0:T(8,128)(2,1)}, bf16[2,8,128,128]{3,2,1,0:T(8,128)(2,1)S(1)}, u32[]{:S(2)}, u32[]{:S(2)}) collective-permute-start(bf16[2,8,128,128]{3,2,1,0:T(8,128)(2,1)} %get-tuple-element.16), channel_id=1, source_target_pairs={{0,32},{32,64},{64,96},{96,128},{128,160},{160,192},{192,224},{1,3... | collective-permute-start | bytes 1572872 | tf_op jit(solution)/shard_map/ppermute | solution.py:396
  72.8 1.2 %copy-start = (f32[2,1536,128]{2,1,0:T(8,128)}, f32[2,1536,128]{2,1,0:T(8,128)S(1)}, u32[]{:S(2)}) copy-start(f32[2,1536,128]{2,1,0:T(8,128)S(1)} %get-tuple-element.17.refs_2_.mixed_in) | copy-start | bytes 4718596
  73.9 1.1 copy-start.3
  81.9 1.4 %copy-start.1 = (f32[2,1536,128]{2,1,0:T(8,128)S(1)}, f32[2,1536,128]{2,1,0:T(8,128)}, u32[]{:S(2)}) copy-start(f32[2,1536,128]{2,1,0:T(8,128)} %copy-done) | copy-start | bytes 4718596
  83.3 4.2 %copy-start.2 = (f32[2,1536,128]{2,1,0:T(8,128)S(1)}, f32[2,1536,128]{2,1,0:T(8,128)}, u32[]{:S(2)}) copy-start(f32[2,1536,128]{2,1,0:T(8,128)} %copy-done) | copy-start | bytes 4718596
  83.4 4.2 %copy-start.4 = (f32[2,1536,128]{2,1,0:T(8,128)S(1)}, f32[2,1536,128]{2,1,0:T(8,128)}, u32[]{:S(2)}) copy-start(f32[2,1536,128]{2,1,0:T(8,128)} %copy-done.3) | copy-start | bytes 4718596
  83.4 4.2 %collective-permute-start.5 = (bf16[2,8,384,128]{3,2,1,0:T(8,128)(2,1)S(1)}, bf16[2,8,384,128]{3,2,1,0:T(8,128)(2,1)S(1)}, u32[]{:S(2)}, u32[]{:S(2)}) collective-permute-start(bf16[2,8,384,128]{3,2,1,0:T(8,128)(2,1)S(1)} %get-tuple-element.19.v_back), channel_id=1, source_target_pairs={{0,8},{8,0},{1,9},{9,1},{2,10},{10,2},{3,11},{11,3},{4,12},{12,4},... | collective-permute-start | bytes 4718600 | tf_op jit(solution)/shard_map/ppermute | solution.py:400
  83.4 4.2 %collective-permute-start.4 = (bf16[2,8,128,128]{3,2,1,0:T(8,128)(2,1)S(1)}, bf16[2,8,128,128]{3,2,1,0:T(8,128)(2,1)S(1)}, u32[]{:S(2)}, u32[]{:S(2)}) collective-permute-start(bf16[2,8,128,128]{3,2,1,0:T(8,128)(2,1)S(1)} %get-tuple-element.18.k_back), channel_id=1, source_target_pairs={{0,8},{8,0},{1,9},{9,1},{2,10},{10,2},{3,11},{11,3},{4,12},{12,4},... | collective-permute-start | bytes 1572872 | tf_op jit(solution)/shard_map/ppermute | solution.py:400
